TPU v7x, 32 devices: a whole 2x2x4 slice. The times are simulated.
32 devices in a mesh: path: 16 (over z, y, x), shard: 2 (over core).
Axes of the slice: x: 2, y: 2, z: 4, core: 2. Of those that a mesh axis runs over, the one named last changes fastest.
Arguments:
- features: bfloat16 [16, 512, 768], P('path', None, 'shard'), may hold values from -6 to 6
- path_weights: bfloat16 [16, 768, 3072], P('path', None, 'shard'), may hold values from -6 to 6
- cotangent: bfloat16 [16, 512, 3072], P('path', None, 'shard'), may hold values from -6 to 6
- path_module: int32 [16, 1], replicated, may hold values from 0 to 15
- outer_params: float32 [16, 768, 3072], P(None, 'path', 'shard'), may hold values from -6 to 6
- outer_moment: float32 [16, 768, 3072], P(None, 'path', 'shard'), may hold values from -2 to 2
Outputs:
- synced: bfloat16 [16, 768, 3072], P('path', None, 'shard')
- params_new: float32 [16, 768, 3072], P(None, 'path', 'shard')
- moment_new: float32 [16, 768, 3072], P(None, 'path', 'shard')
- grad_weight: bfloat16 [16, 768, 3072], P('path', None, 'shard')
- grad_input: bfloat16 [16, 512, 768], P('path', None, 'shard')
Inputs may be any that keep to these rules, and one draw needn't show every extreme that they name: `path_module`: every module id is used by at least one path.
All inputs are finite; a program needn't handle non-finite values.
Results may differ from a plain program's by a relative error of at most 0.005.
Values may be sent and summed in bfloat16 or wider, within the bound.
A program may use at most 64 MiB of HBM per device.

v0:
```python
import jax
import jax.numpy as jnp
from jax import lax
from jax.sharding import PartitionSpec as P

D = 768
MODULES = 16


outer_momentum = 0.9
outer_rate = 0.7


def silu_slope(pre):
    sigmoid_part = jax.nn.sigmoid(pre)
    return sigmoid_part * (1.0 + pre * (1.0 - sigmoid_part))


def on_device(features, path_weights, cotangent, path_module, outer_params, outer_moment):
    multiplier = D ** (-0.5)
    weights_here = path_weights[0]
    count_path = lax.axis_size("path")
    received = lax.all_to_all(weights_here, "path", split_axis=0, concat_axis=0, tiled=True)
    flattened = received.reshape(count_path, -1)
    modules = path_module[:, 0]
    member = modules[None, :] == jnp.arange(MODULES, dtype=jnp.int32)[:, None]
    summed = jnp.dot(member.astype(jnp.bfloat16), flattened, preferred_element_type=jnp.float32)
    counts = jnp.sum(member.astype(jnp.float32), axis=1)
    average = summed / counts[:, None]
    shaped = outer_params.reshape(MODULES, -1)
    pseudo = shaped - average
    moment_flat = outer_momentum * outer_moment.reshape(MODULES, -1) + pseudo
    params_flat = shaped - outer_rate * (pseudo + outer_momentum * moment_flat)
    chosen = jnp.dot(
        member.T.astype(jnp.bfloat16),
        params_flat.astype(jnp.bfloat16),
        preferred_element_type=jnp.float32,
    )
    chosen = chosen.astype(jnp.bfloat16).reshape(received.shape)
    returned = lax.all_to_all(chosen, "path", split_axis=0, concat_axis=0, tiled=True)
    synced = returned[None]
    params_new = params_flat.reshape(outer_params.shape)
    moment_new = moment_flat.reshape(outer_moment.shape)
    tokens_full = lax.all_gather(features, "shard", axis=2, tiled=True)[0]
    pre = jnp.dot(tokens_full, weights_here, preferred_element_type=jnp.float32) * multiplier
    delta = (cotangent[0].astype(jnp.float32) * silu_slope(pre)).astype(jnp.bfloat16)
    grad_w = lax.dot_general(
        tokens_full, delta, (((0,), (0,)), ((), ())), preferred_element_type=jnp.float32
    )
    grad_w = (grad_w * multiplier).astype(jnp.bfloat16)
    terms = lax.dot_general(
        delta, weights_here, (((1,), (1,)), ((), ())), preferred_element_type=jnp.float32
    )
    terms = terms * multiplier
    whole = lax.psum(terms, "shard")
    width = terms.shape[1] // lax.axis_size("shard")
    grad_in = lax.dynamic_slice_in_dim(whole, lax.axis_index("shard") * width, width, 1).astype(
        jnp.bfloat16
    )
    grad_weight = grad_w[None]
    grad_input = grad_in[None]
    return (synced, params_new, moment_new, grad_weight, grad_input)


def solution(mesh):
    return jax.shard_map(
        on_device,
        mesh=mesh,
        in_specs=(
            P("path", None, "shard"),
            P("path", None, "shard"),
            P("path", None, "shard"),
            P(),
            P(None, "path", "shard"),
            P(None, "path", "shard"),
        ),
        out_specs=(
            P("path", None, "shard"),
            P(None, "path", "shard"),
            P(None, "path", "shard"),
            P("path", None, "shard"),
            P("path", None, "shard"),
        ),
        check_vma=False,
    )
```

profile of v0, /device:TPU:12, one launch (start us, length us, event | category | flops | bytes accessed | tf_op | source)
XLA Modules:
  0.0 133.9 jit_solution(1994398098545287056)
XLA Ops:
  0.6 7.2 %all-to-all-start = ((bf16[16,48,1536]{2,1,0:T(8,128)(2,1)}), bf16[16,48,1536]{2,1,0:T(8,128)(2,1)S(1)}, u32[]{:S(2)}, u32[]{:S(2)}) async-start(bf16[16,48,1536]{2,1,0:T(8,128)(2,1)} %bitcast.57), calls=%async_computation | async-start | bytes 4718592 | tf_op jit(solution)/shard_map/all_to_all | solution.py:23
  7.8 2.9 %broadcast_multiply_fusion = f32[16,48,1536]{2,1,0:T(8,128)S(1)} fusion(f32[16,48,1536]{2,1,0:T(8,128)} %param.11), kind=kLoop, calls=%fused_computation.13 | loop fusion | flops 1179648 | bytes 9437184 | tf_op jit(solution)/shard_map/mul | solution.py:32
  10.7 0.0 slice-start
  10.7 0.0 slice-start.1
  10.8 4.9 %copy.15 = f32[2,8,48,1536]{3,1,2,0:T(8,128)} copy(f32[2,8,48,1536]{3,2,1,0:T(8,128)S(1)} %bitcast.42) | data formatting | bytes 9437184
  15.7 0.0 slice-done
  15.7 0.0 slice-done.1
  15.7 0.0 copy-start.4
  15.7 4.9 %copy.13 = f32[2,8,48,1536]{3,1,2,0:T(8,128)} copy(f32[2,8,48,1536]{3,2,1,0:T(8,128)S(1)} %bitcast.49) | data formatting | bytes 9437184
  20.6 0.0 copy-done.4
  20.6 0.1 convert_reduce_fusion
  20.7 40.8 %all-to-all-done = bf16[16,48,1536]{2,1,0:T(8,128)(2,1)S(1)} async-done(((bf16[16,48,1536]{2,1,0:T(8,128)(2,1)}), bf16[16,48,1536]{2,1,0:T(8,128)(2,1)S(1)}, u32[]{:S(2)}, u32[]{:S(2)}) %all-to-all-start) | async-done | bytes 2359328 | tf_op jit(solution)/shard_map/all_to_all | solution.py:23
  61.5 0.0 copy-start.1
  61.5 1.3 copy.14
  62.8 1.0 copy-done.1
  63.9 6.2 %multiply_subtract_fusion = (f32[16,73728]{1,0:T(8,128)S(1)}, f32[16,73728]{1,0:T(8,128)}) fusion(f32[16,73728]{1,0:T(8,128)} %bitcast.56, f32[16,73728]{1,0:T(8,128)S(1)} %bitcast.55, f32[16]{0:T(128)S(1)} %convert_reduce_fusion, bf16[16,73728]{1,0:T(8,128)(2,1)S(1)} %bitcast.58, s32[16]{0:T(128)S(1)} %bitcast.60), kind=kOutput, calls=%fused_computation.4 | convolution fusion | flops 46006528 | bytes 21233792 | tf_op jit(solution)/shard_map/dot_general | solution.py:27
  70.1 0.0 copy-start
  70.1 1.0 convolution_convert_fusion
  71.2 1.1 copy-done
  72.2 2.1 %copy.16 = bf16[2,8,48,1536]{3,2,1,0:T(8,128)(2,1)} copy(bf16[2,8,48,1536]{3,1,2,0:T(8,128)(2,1)S(1)} %bitcast.43) | data formatting | bytes 4718592
  74.3 0.0 copy-start.3
  74.3 5.0 %all-to-all-start.1 = ((bf16[16,48,1536]{2,1,0:T(8,128)(2,1)}), bf16[16,48,1536]{2,1,0:T(8,128)(2,1)S(1)}, u32[]{:S(2)}, u32[]{:S(2)}) async-start(bf16[16,48,1536]{2,1,0:T(8,128)(2,1)} %bitcast.45), calls=%async_computation.1 | async-start | bytes 4718592 | tf_op jit(solution)/shard_map/all_to_all | solution.py:40
  79.4 0.0 copy-done.3
  79.4 2.5 %all_gather.3 = bf16[1,512,768]{2,1,0:T(8,128)(2,1)S(1)} all-gather(bf16[1,512,384]{2,1,0:T(8,128)(2,1)S(1)} %copy-done.3), channel_id=1, replica_groups=mesh['path'=16,'shard'=2] {'shard'}, dimensions={2}, use_global_device_ids=true | all-gather | bytes 1179648 | tf_op jit(solution)/shard_map/all_gather | solution.py:44
  81.9 0.0 copy-start.2
  81.9 4.5 %fusion.1 = bf16[512,1536]{1,0:T(8,128)(2,1)S(1)} fusion(bf16[1,768,1536]{2,1,0:T(8,128)(2,1)} %param.7, bf16[1,512,1536]{2,1,0:T(8,128)(2,1)} %param.8, bf16[1,512,768]{2,1,0:T(8,128)(2,1)S(1)} %all_gather.3), kind=kOutput, calls=%fused_computation.7 | convolution fusion | flops 1216610304 | bytes 6291456 | tf_op jit(solution)/shard_map/dot_general | solution.py:45
  86.4 0.0 copy-done.2
  86.4 2.6 %fusion.9 = f32[512,768]{1,0:T(8,128)} fusion(bf16[512,1536]{1,0:T(8,128)(2,1)S(1)} %fusion.1, bf16[1,768,1536]{2,1,0:T(8,128)(2,1)S(1)} %copy-done.2), kind=kOutput, calls=%fused_computation.14 | convolution fusion | flops 1208352768 | bytes 5505024 | tf_op jit(solution)/shard_map/dot_general | solution.py:51
  89.0 2.8 %fusion.2 = bf16[1,768,1536]{1,2,0:T(8,128)(2,1)} fusion(bf16[512,1536]{1,0:T(8,128)(2,1)S(1)} %fusion.1, bf16[1,512,768]{2,1,0:T(8,128)(2,1)S(1)} %all_gather.3), kind=kOutput, calls=%fused_computation.8 | convolution fusion | flops 1210318848 | bytes 4718592 | tf_op jit(solution)/shard_map/dot_general | solution.py:47
  91.8 4.3 %copy.12 = bf16[1,768,1536]{2,1,0:T(8,128)(2,1)} copy(bf16[1,768,1536]{1,2,0:T(8,128)(2,1)} %fusion.2) | data formatting | bytes 4718592
  96.1 8.3 %all-reduce.1 = bf16[512,768]{1,0:T(8,128)(2,1)S(1)} all-reduce(f32[512,768]{1,0:T(8,128)} %fusion.9), channel_id=1, replica_groups=mesh['path'=16,'shard'=2] {'shard'}, use_global_device_ids=true, to_apply=%region_1.0 | all-reduce | flops 393216 | bytes 2359296 | tf_op jit(solution)/shard_map/psum | solution.py:55
  104.4 0.8 fusion.14
  105.2 0.0 slice-start.2
  105.2 0.0 slice-start.3
  105.2 7.4 %copy.17 = f32[2,8,48,1536]{3,2,1,0:T(8,128)} copy(f32[2,8,48,1536]{3,1,2,0:T(8,128)} %bitcast.41) | data formatting | bytes 9437184
  112.6 0.0 slice-done.2
  112.6 0.0 slice-done.3
  112.6 4.9 %copy.18 = f32[2,8,48,1536]{3,2,1,0:T(8,128)} copy(f32[2,8,48,1536]{3,1,2,0:T(8,128)S(1)} %bitcast.52) | data formatting | bytes 9437184
  117.5 15.0 %all-to-all-done.1 = bf16[16,48,1536]{2,1,0:T(8,128)(2,1)S(1)} async-done(((bf16[16,48,1536]{2,1,0:T(8,128)(2,1)}), bf16[16,48,1536]{2,1,0:T(8,128)(2,1)S(1)}, u32[]{:S(2)}, u32[]{:S(2)}) %all-to-all-start.1) | async-done | bytes 2359328 | tf_op jit(solution)/shard_map/all_to_all | solution.py:40
  132.5 1.4 %copy.22 = bf16[1,768,1536]{2,1,0:T(8,128)(2,1)} copy(bf16[1,768,1536]{2,1,0:T(8,128)(2,1)S(1)} %bitcast.44) | data formatting | bytes 4718592
  (2 shorter events, 0.0 us)
Async XLA Ops:
  0.6 60.9 %all-to-all-start = ((bf16[16,48,1536]{2,1,0:T(8,128)(2,1)}), bf16[16,48,1536]{2,1,0:T(8,128)(2,1)S(1)}, u32[]{:S(2)}, u32[]{:S(2)}) async-start(bf16[16,48,1536]{2,1,0:T(8,128)(2,1)} %bitcast.57), calls=%async_computation | async-start | bytes 4718592 | tf_op jit(solution)/shard_map/all_to_all | solution.py:23
  10.7 4.9 %slice-start = ((s8[4718592]{0:T(1024)(128)(4,1)}), s8[4194304]{0:T(1024)(128)(4,1)S(1)}, s32[]{:S(2)}) async-start(s8[4718592]{0:T(1024)(128)(4,1)} %bitcast.47), calls=%async_computation.2 | async-start | bytes 8388608
  10.7 4.9 %slice-start.1 = ((s8[4718592]{0:T(1024)(128)(4,1)}), s8[524288]{0:T(1024)(128)(4,1)S(1)}, s32[]{:S(2)}) async-start(s8[4718592]{0:T(1024)(128)(4,1)} %bitcast.47), calls=%async_computation.3 | async-start | bytes 1048576
  15.7 4.9 %copy-start.4 = (s32[16,1]{0,1:T(1,128)S(1)}, s32[16,1]{0,1:T(1,128)}, u32[]{:S(2)}) copy-start(s32[16,1]{0,1:T(1,128)} %param.9) | copy-start | bytes 196
  61.5 2.3 %copy-start.1 = (f32[2,8,48,1536]{3,1,2,0:T(8,128)S(1)}, f32[2,8,48,1536]{3,1,2,0:T(8,128)}, u32[]{:S(2)}) copy-start(f32[2,8,48,1536]{3,1,2,0:T(8,128)} %copy.15) | copy-start | bytes 14155780
  70.1 2.1 %copy-start = (f32[16,73728]{1,0:T(8,128)}, f32[16,73728]{1,0:T(8,128)S(1)}, u32[]{:S(2)}) copy-start(f32[16,73728]{1,0:T(8,128)S(1)} %get-tuple-element.15) | copy-start | bytes 14155780
  74.3 5.0 %copy-start.3 = (bf16[1,512,384]{2,1,0:T(8,128)(2,1)S(1)}, bf16[1,512,384]{2,1,0:T(8,128)(2,1)}, u32[]{:S(2)}) copy-start(bf16[1,512,384]{2,1,0:T(8,128)(2,1)} %param.6) | copy-start | bytes 1179652
  74.3 58.1 %all-to-all-start.1 = ((bf16[16,48,1536]{2,1,0:T(8,128)(2,1)}), bf16[16,48,1536]{2,1,0:T(8,128)(2,1)S(1)}, u32[]{:S(2)}, u32[]{:S(2)}) async-start(bf16[16,48,1536]{2,1,0:T(8,128)(2,1)} %bitcast.45), calls=%async_computation.1 | async-start | bytes 4718592 | tf_op jit(solution)/shard_map/all_to_all | solution.py:40
  81.9 4.5 %copy-start.2 = (bf16[1,768,1536]{2,1,0:T(8,128)(2,1)S(1)}, bf16[1,768,1536]{2,1,0:T(8,128)(2,1)}, u32[]{:S(2)}) copy-start(bf16[1,768,1536]{2,1,0:T(8,128)(2,1)} %param.7) | copy-start | bytes 7077892
  105.2 7.4 %slice-start.2 = ((s8[4718592]{0:T(1024)(128)(4,1)}), s8[4194304]{0:T(1024)(128)(4,1)S(1)}, s32[]{:S(2)}) async-start(s8[4718592]{0:T(1024)(128)(4,1)} %bitcast.50), calls=%async_computation.4 | async-start | bytes 8388608
  105.2 7.4 %slice-start.3 = ((s8[4718592]{0:T(1024)(128)(4,1)}), s8[524288]{0:T(1024)(128)(4,1)S(1)}, s32[]{:S(2)}) async-start(s8[4718592]{0:T(1024)(128)(4,1)} %bitcast.50), calls=%async_computation.5 | async-start | bytes 1048576
where the time goes:
time: 134 us
  waiting for transfers between devices  55.8 us (42%)
  local copies, waits for them, and re-layouts  34.2 us (26%)
  matrix products  17.2 us (13%)
  starting transfers between devices  12.2 us (9%)
  blocking collectives  10.8 us (8%)
  other arithmetic  3.03 us (2%)
    all_to_all x1, waiting for transfers between devices, on_device(): lax.all_to_all(weights_here, 'path', split_axis=0, concat_axis=0, tiled=T...  40.8 us
    unnamed x26, local copies, waits for them, and re-layouts  33.4 us
    all_to_all x1, waiting for transfers between devices, on_device(): lax.all_to_all(chosen, 'path', split_axis=0, concat_axis=0, tiled=True)  15 us
    psum x1, blocking collectives, on_device(): whole = lax.psum(terms, 'shard')  8.25 us
    all_to_all x1, starting transfers between devices, on_device(): lax.all_to_all(weights_here, 'path', split_axis=0, concat_axis=0, tiled=T...  7.18 us
    dot_general x1, matrix products, on_device(): jnp.dot(member.astype(jnp.bfloat16), flattened, preferred_element_type=jn...  6.23 us
    all_to_all x1, starting transfers between devices, on_device(): lax.all_to_all(chosen, 'path', split_axis=0, concat_axis=0, tiled=True)  5.04 us
    dot_general x1, matrix products, on_device(): jnp.dot(tokens_full, weights_here, preferred_element_type=jnp.float32)  4.48 us
  transfers between devices with their start and end apart: 2, of which 2 were waited for; matrix products, arithmetic and copies ran while one was open for 30% of the time, Pallas kernels for 0%

commit v1 on v0

v1 whole, which is shorter than its diff:
```python
import functools

import jax
import jax.numpy as jnp
from jax import lax
from jax.experimental import pallas as pl
from jax.experimental.pallas import tpu as pltpu
from jax.sharding import PartitionSpec as P

outer_momentum = 0.9
outer_rate = 0.7


def silu_slope(pre):
    sigmoid_part = jax.nn.sigmoid(pre)
    return sigmoid_part * (1.0 + pre * (1.0 - sigmoid_part))


def partner(index, count, flips):
    result = 0
    place = 1
    while place < count:
        bit = lax.rem(lax.div(index, place), 2)
        result = result + place * (1 - bit if flips & place else bit)
        place *= 2
    return result


def send_order(count):
    return sorted(range(1, count), key=lambda flips: (flips < count // 2, flips))


def fused_kernel(
    count,
    module_ref,
    features_hbm,
    weights_hbm,
    cotangent_hbm,
    params_hbm,
    moment_hbm,
    synced_ref,
    params_new_ref,
    moment_new_ref,
    grad_weight_ref,
    grad_input_ref,
    tokens,
    weights,
    cotangent,
    params,
    moment,
    received,
    own,
    returned,
    terms,
    terms_other,
    local_sem,
    out_send,
    out_recv,
    back_send,
    back_recv,
    pair_send,
    pair_recv,
):
    me = lax.axis_index("path")
    core = lax.axis_index("shard")
    other = 1 - core
    rows, columns = params.shape[1:]
    depth = count * rows
    order = send_order(count)

    def block_of(path):
        return pl.ds(pl.multiple_of(path * rows, rows), rows)

    local = [
        pltpu.make_async_copy(params_hbm, params, local_sem.at[0]),
        pltpu.make_async_copy(moment_hbm, moment, local_sem.at[1]),
        pltpu.make_async_copy(weights_hbm, weights, local_sem.at[2]),
        pltpu.make_async_copy(cotangent_hbm, cotangent, local_sem.at[3]),
        pltpu.make_async_copy(features_hbm, tokens.at[core], local_sem.at[4]),
        pltpu.make_async_copy(weights_hbm.at[block_of(me)], received.at[me], local_sem.at[5]),
    ]
    for copy in local:
        copy.start()

    barrier = pltpu.get_barrier_semaphore()
    for flips in order:
        pl.semaphore_signal(barrier, inc=1, device_id={"path": partner(me, count, flips)})
    pl.semaphore_signal(barrier, inc=1, device_id={"shard": other})
    pl.semaphore_wait(barrier, count)

    outward = []
    for flips in order:
        peer = partner(me, count, flips)
        copy = pltpu.make_async_remote_copy(
            src_ref=weights_hbm.at[block_of(peer)],
            dst_ref=received.at[me],
            send_sem=out_send.at[flips],
            recv_sem=out_recv.at[flips],
            device_id={"path": peer},
        )
        copy.start()
        outward.append(copy)
    give_tokens = pltpu.make_async_remote_copy(
        src_ref=features_hbm,
        dst_ref=tokens.at[core],
        send_sem=pair_send.at[0],
        recv_sem=pair_recv.at[0],
        device_id={"shard": other},
    )
    give_tokens.start()

    local[0].wait()
    local[1].wait()

    def own_block(path):
        at = module_ref[path]
        shaped = params[at]
        moved = outer_momentum * moment[at] + shaped
        return shaped - outer_rate * (shaped + outer_momentum * moved)

    @pl.loop(0, count)
    def _(path):
        own[path] = own_block(path).astype(own.dtype)

    back = []
    for flips in order:
        peer = partner(me, count, flips)
        copy = pltpu.make_async_remote_copy(
            src_ref=own.at[peer],
            dst_ref=returned.at[me],
            send_sem=back_send.at[flips],
            recv_sem=back_recv.at[flips],
            device_id={"path": peer},
        )
        copy.start()
        back.append(copy)

    share = outer_rate * (1.0 + outer_momentum)
    for copy in local[2:]:
        copy.wait()
    synced_ref[block_of(me), :] = (
        own_block(me) + share * weights[block_of(me), :].astype(jnp.float32)
    ).astype(synced_ref.dtype)
    give_tokens.wait()

    multiplier = depth ** (-0.5)
    half = depth // 2
    tile = 256
    terms[...] = jnp.zeros_like(terms)

    @pl.loop(0, columns // tile)
    def _(step):
        cols = pl.ds(pl.multiple_of(step * tile, tile), tile)
        pre = jnp.dot(tokens[0], weights[:half, cols], preferred_element_type=jnp.float32)
        pre += jnp.dot(tokens[1], weights[half:, cols], preferred_element_type=jnp.float32)
        slope = silu_slope(pre * multiplier)
        delta = (cotangent[:, cols].astype(jnp.float32) * slope).astype(jnp.bfloat16)
        for part in range(2):
            grad = lax.dot_general(
                tokens[part], delta, (((0,), (0,)), ((), ())), preferred_element_type=jnp.float32
            )
            grad_weight_ref[part * half : (part + 1) * half, cols] = (grad * multiplier).astype(
                grad_weight_ref.dtype
            )
            terms[part] += lax.dot_general(
                delta,
                weights[part * half : (part + 1) * half, cols],
                (((1,), (1,)), ((), ())),
                preferred_element_type=jnp.float32,
            )

    give_terms = pltpu.make_async_remote_copy(
        src_ref=terms.at[other],
        dst_ref=terms_other,
        send_sem=pair_send.at[1],
        recv_sem=pair_recv.at[1],
        device_id={"shard": other},
    )
    give_terms.start()
    give_terms.wait()
    grad_input_ref[...] = ((terms[core] + terms_other[...]) * multiplier).astype(
        grad_input_ref.dtype
    )

    for copy in outward:
        copy.wait()

    @pl.loop(0, count)
    def _(at):
        path = lax.fori_loop(
            0, count, lambda i, found: jnp.where(module_ref[i] == at, i, found), jnp.int32(0)
        )
        shaped = params[at]
        pseudo = shaped - received[path].astype(jnp.float32)
        moved = outer_momentum * moment[at] + pseudo
        moment_new_ref[at] = moved
        params_new_ref[at] = shaped - outer_rate * (pseudo + outer_momentum * moved)

    for flips, copy in zip(order, back):
        copy.wait()
        peer = partner(me, count, flips)
        synced_ref[block_of(peer), :] = (
            returned[peer].astype(jnp.float32)
            + share * weights[block_of(peer), :].astype(jnp.float32)
        ).astype(synced_ref.dtype)


def fused(features, weights_here, cotangent, path_module, outer_params, outer_moment):
    count, rows, columns = outer_params.shape
    depth = weights_here.shape[0]
    tokens, half = features.shape
    anywhere = pl.BlockSpec(memory_space=pl.ANY)
    sixteen = jnp.bfloat16
    return pl.pallas_call(
        functools.partial(fused_kernel, count),
        in_specs=[pl.BlockSpec(memory_space=pltpu.SMEM)] + [anywhere] * 5,
        out_specs=[pl.BlockSpec(memory_space=pltpu.VMEM)] * 5,
        out_shape=[
            pltpu.VMEM((depth, columns), sixteen),
            pltpu.VMEM(outer_params.shape, jnp.float32),
            pltpu.VMEM(outer_params.shape, jnp.float32),
            pltpu.VMEM((depth, columns), sixteen),
            pltpu.VMEM((tokens, half), sixteen),
        ],
        scratch_shapes=[
            pltpu.VMEM((2, tokens, half), sixteen),
            pltpu.VMEM((depth, columns), sixteen),
            pltpu.VMEM((tokens, columns), sixteen),
            pltpu.VMEM(outer_params.shape, jnp.float32),
            pltpu.VMEM(outer_params.shape, jnp.float32),
            pltpu.VMEM(outer_params.shape, sixteen),
            pltpu.VMEM(outer_params.shape, sixteen),
            pltpu.VMEM(outer_params.shape, sixteen),
            pltpu.VMEM((2, tokens, half), jnp.float32),
            pltpu.VMEM((tokens, half), jnp.float32),
            pltpu.SemaphoreType.DMA((6,)),
            pltpu.SemaphoreType.DMA((count,)),
            pltpu.SemaphoreType.DMA((count,)),
            pltpu.SemaphoreType.DMA((count,)),
            pltpu.SemaphoreType.DMA((count,)),
            pltpu.SemaphoreType.DMA((2,)),
            pltpu.SemaphoreType.DMA((2,)),
        ],
        compiler_params=pltpu.CompilerParams(
            collective_id=0, has_side_effects=True, vmem_limit_bytes=40 * 2**20
        ),
    )(path_module[:, 0], features, weights_here, cotangent, outer_params, outer_moment)


def many_paths_each(weights_here, path_module, outer_params, outer_moment):
    count_path = lax.axis_size("path")
    module_count = outer_params.shape[0]
    received = lax.all_to_all(weights_here, "path", split_axis=0, concat_axis=0, tiled=True)
    flattened = received.reshape(count_path, -1)
    modules = path_module[:, 0]
    member = modules[None, :] == jnp.arange(module_count, dtype=jnp.int32)[:, None]
    summed = jnp.dot(member.astype(jnp.bfloat16), flattened, preferred_element_type=jnp.float32)
    counts = jnp.sum(member.astype(jnp.float32), axis=1)
    average = summed / counts[:, None]
    shaped = outer_params.reshape(module_count, -1)
    pseudo = shaped - average
    moment_flat = outer_momentum * outer_moment.reshape(module_count, -1) + pseudo
    params_flat = shaped - outer_rate * (pseudo + outer_momentum * moment_flat)
    chosen = jnp.dot(
        member.T.astype(jnp.bfloat16),
        params_flat.astype(jnp.bfloat16),
        preferred_element_type=jnp.float32,
    )
    chosen = chosen.astype(jnp.bfloat16).reshape(received.shape)
    returned = lax.all_to_all(chosen, "path", split_axis=0, concat_axis=0, tiled=True)
    return returned, params_flat.reshape(outer_params.shape), moment_flat.reshape(outer_moment.shape)


def inner_layer(features, weights_here, cotangent):
    tokens_full = lax.all_gather(features, "shard", axis=1, tiled=True)
    multiplier = tokens_full.shape[1] ** (-0.5)
    pre = jnp.dot(tokens_full, weights_here, preferred_element_type=jnp.float32) * multiplier
    delta = (cotangent.astype(jnp.float32) * silu_slope(pre)).astype(jnp.bfloat16)
    grad_w = lax.dot_general(
        tokens_full, delta, (((0,), (0,)), ((), ())), preferred_element_type=jnp.float32
    )
    grad_w = (grad_w * multiplier).astype(jnp.bfloat16)
    terms = lax.dot_general(
        delta, weights_here, (((1,), (1,)), ((), ())), preferred_element_type=jnp.float32
    )
    terms = terms * multiplier
    whole = lax.psum(terms, "shard")
    width = terms.shape[1] // lax.axis_size("shard")
    grad_in = lax.dynamic_slice_in_dim(whole, lax.axis_index("shard") * width, width, 1)
    return grad_w, grad_in.astype(jnp.bfloat16)


def fits_fused(weights_here, outer_params):
    count, rows, columns = outer_params.shape
    return (
        lax.axis_size("path") == count
        and count & (count - 1) == 0
        and lax.axis_size("shard") == 2
        and rows % 16 == 0
        and columns % 256 == 0
        and (count * rows) % 256 == 0
    )


def on_device(features, path_weights, cotangent, path_module, outer_params, outer_moment):
    weights_here = path_weights[0]
    if fits_fused(weights_here, outer_params):
        synced, params_new, moment_new, grad_weight, grad_input = fused(
            features[0], weights_here, cotangent[0], path_module, outer_params, outer_moment
        )
    else:
        synced, params_new, moment_new = many_paths_each(
            weights_here, path_module, outer_params, outer_moment
        )
        grad_weight, grad_input = inner_layer(features[0], weights_here, cotangent[0])
    return (synced[None], params_new, moment_new, grad_weight[None], grad_input[None])


def solution(mesh):
    return jax.shard_map(
        on_device,
        mesh=mesh,
        in_specs=(
            P("path", None, "shard"),
            P("path", None, "shard"),
            P("path", None, "shard"),
            P(),
            P(None, "path", "shard"),
            P(None, "path", "shard"),
        ),
        out_specs=(
            P("path", None, "shard"),
            P(None, "path", "shard"),
            P(None, "path", "shard"),
            P("path", None, "shard"),
            P("path", None, "shard"),
        ),
        check_vma=False,
    )
```

time: 134 us -> 125 us (0.933)
  Pallas kernels: 0 us -> 115 us
  waiting for transfers between devices: 55.8 us -> 0 us
  local copies, waits for them, and re-layouts: 34.2 us -> 8.58 us
  matrix products: 17.2 us -> 0 us
  starting transfers between devices: 12.2 us -> 0 us
  blocking collectives: 10.8 us -> 0 us
  other arithmetic: 3.03 us -> 0 us
    pallas_call x0 -> x1, Pallas kernels: none -> 115 us  [fused(): pl.pallas_call(functools.partial(fused_kernel, count), in_specs=[pl.Block...]
    all_to_all x2 -> x0, waiting for transfers between devices: 55.8 us -> none  [the longest x1 40.8 us: on_device(): lax.all_to_all(weights_here, 'path', split_axis=0, concat_axis=0, tiled=T...]
    unnamed x26 -> x7, local copies, waits for them, and re-layouts: 33.4 us -> 8.58 us
    dot_general x5 -> x0, matrix products: 17.2 us -> none  [the longest x1 6.23 us: on_device(): jnp.dot(member.astype(jnp.bfloat16), flattened, preferred_element_type=jn...]
    all_to_all x2 -> x0, starting transfers between devices: 12.2 us -> none  [the longest x1 7.18 us: on_device(): lax.all_to_all(weights_here, 'path', split_axis=0, concat_axis=0, tiled=T...]
    psum x1 -> x0, blocking collectives: 8.25 us -> none  [on_device(): whole = lax.psum(terms, 'shard')]
    mul x1 -> x0, other arithmetic: 2.92 us -> none  [on_device(): moment_flat = outer_momentum * outer_moment.reshape(MODULES, -1) + pseudo]
    all_gather x1 -> x0, blocking collectives: 2.55 us -> none  [on_device(): tokens_full = lax.all_gather(features, 'shard', axis=2, tiled=True)[0]]
  transfers between devices with their start and end apart: 2 -> 0, of which waited for: 2 -> 0; matrix products, arithmetic and copies ran while one was open for 30% -> 0% of each run, Pallas kernels for 0% -> 0%
where the time goes in v1:
time: 125 us
  Pallas kernels  115 us (92%)
  local copies, waits for them, and re-layouts  8.58 us (7%)
    pallas_call x1, Pallas kernels, fused(): pl.pallas_call(functools.partial(fused_kernel, count), in_specs=[pl.Block...  115 us
    unnamed x7, local copies, waits for them, and re-layouts  8.58 us

profile of v1, /device:TPU:12, one launch (start us, length us, event | category | flops | bytes accessed | tf_op | source)
XLA Modules:
  0.0 124.6 jit_solution(5618336402648560563)
XLA Ops:
  0.6 0.0 copy-start
  0.6 0.6 copy-done
  1.3 115.4 %shard_map.101 = (bf16[768,1536]{1,0:T(8,128)(2,1)S(1)}, f32[16,48,1536]{2,1,0:T(8,128)S(1)}, f32[16,48,1536]{2,1,0:T(8,128)S(1)}, bf16[768,1536]{1,0:T(8,128)(2,1)S(1)}, bf16[512,384]{1,0:T(8,128)(2,1)S(1)}) custom-call(s32[16]{0:T(128)S(1)} %bitcast.10, bf16[512,384]{1,0:T(8,128)(2,1)} %bitcast.13, bf16[768,1536]{1,0:T(8,128)(2,1)} %bitcast.11, ...), custom_call_target="tpu_custom_call" | custom-call | tf_op jit(solution)/shard_map/pallas_call | solution.py:214
  116.7 1.4 %copy.16 = bf16[1,768,1536]{2,1,0:T(8,128)(2,1)} copy(bf16[1,768,1536]{2,1,0:T(8,128)(2,1)S(1)} %bitcast.8) | data formatting | bytes 4718592
  118.1 0.7 copy.20
  118.8 1.4 %copy.19 = bf16[1,768,1536]{2,1,0:T(8,128)(2,1)} copy(bf16[1,768,1536]{2,1,0:T(8,128)(2,1)S(1)} %bitcast.7) | data formatting | bytes 4718592
  120.2 2.2 %copy.17 = f32[16,48,1536]{2,1,0:T(8,128)} copy(f32[16,48,1536]{2,1,0:T(8,128)S(1)} %get-tuple-element.16) | data formatting | bytes 9437184
  122.4 2.2 %copy.18 = f32[16,48,1536]{2,1,0:T(8,128)} copy(f32[16,48,1536]{2,1,0:T(8,128)S(1)} %get-tuple-element.17) | data formatting | bytes 9437184
Async XLA Ops:
  0.6 0.7 copy-start

commit v2 on v1

--- a/solution.py
+++ b/solution.py
@@ -21,18 +21,22 @@
     place = 1
     while place < count:
         bit = lax.rem(lax.div(index, place), 2)
-        result = result + place * (1 - bit if flips & place else bit)
+        flip = lax.rem(lax.div(flips, place), 2)
+        result = result + place * (bit + flip - 2 * bit * flip)
         place *= 2
     return result
 
 
-def send_order(count):
-    return sorted(range(1, count), key=lambda flips: (flips < count // 2, flips))
+def send_plan(count):
+    far = range(count // 2, count)
+    near = range(1, count // 2)
+    order = [k for pair in zip(far, near) for k in pair] + [count - 1]
+    return [(kind, k, k) for kind in ("out", "back") for k in order]
 
 
 def fused_kernel(
     count,
-    module_ref,
+    module_hbm,
     features_hbm,
     weights_hbm,
     cotangent_hbm,
@@ -43,6 +47,7 @@
     moment_new_ref,
     grad_weight_ref,
     grad_input_ref,
+    module_ref,
     tokens,
     weights,
     cotangent,
@@ -66,12 +71,13 @@
     other = 1 - core
     rows, columns = params.shape[1:]
     depth = count * rows
-    order = send_order(count)
+    plan = send_plan(count)
 
     def block_of(path):
         return pl.ds(pl.multiple_of(path * rows, rows), rows)
 
     local = [
+        pltpu.make_async_copy(module_hbm, module_ref, local_sem.at[6]),
         pltpu.make_async_copy(params_hbm, params, local_sem.at[0]),
         pltpu.make_async_copy(moment_hbm, moment, local_sem.at[1]),
         pltpu.make_async_copy(weights_hbm, weights, local_sem.at[2]),
@@ -79,27 +85,13 @@
         pltpu.make_async_copy(features_hbm, tokens.at[core], local_sem.at[4]),
         pltpu.make_async_copy(weights_hbm.at[block_of(me)], received.at[me], local_sem.at[5]),
     ]
-    for copy in local:
-        copy.start()
-
     barrier = pltpu.get_barrier_semaphore()
-    for flips in order:
-        pl.semaphore_signal(barrier, inc=1, device_id={"path": partner(me, count, flips)})
+    for flips in range(1, count):
+        peer = partner(me, count, jnp.int32(flips))
+        pl.semaphore_signal(barrier, inc=1, device_id={"path": peer})
     pl.semaphore_signal(barrier, inc=1, device_id={"shard": other})
     pl.semaphore_wait(barrier, count)
 
-    outward = []
-    for flips in order:
-        peer = partner(me, count, flips)
-        copy = pltpu.make_async_remote_copy(
-            src_ref=weights_hbm.at[block_of(peer)],
-            dst_ref=received.at[me],
-            send_sem=out_send.at[flips],
-            recv_sem=out_recv.at[flips],
-            device_id={"path": peer},
-        )
-        copy.start()
-        outward.append(copy)
     give_tokens = pltpu.make_async_remote_copy(
         src_ref=features_hbm,
         dst_ref=tokens.at[core],
@@ -107,36 +99,51 @@
         recv_sem=pair_recv.at[0],
         device_id={"shard": other},
     )
-    give_tokens.start()
-
-    local[0].wait()
-    local[1].wait()
 
     def own_block(path):
-        at = module_ref[path]
+        at = module_ref[0, path]
         shaped = params[at]
         moved = outer_momentum * moment[at] + shaped
         return shaped - outer_rate * (shaped + outer_momentum * moved)
 
-    @pl.loop(0, count)
-    def _(path):
-        own[path] = own_block(path).astype(own.dtype)
-
-    back = []
-    for flips in order:
+    outward, back = [], []
+    for exchange, first, second in plan:
+        flips = first + core * jnp.int32(second - first)
         peer = partner(me, count, flips)
+        if exchange == "out":
+            copy = pltpu.make_async_remote_copy(
+                src_ref=weights_hbm.at[block_of(peer)],
+                dst_ref=received.at[me],
+                send_sem=out_send.at[len(outward)],
+                recv_sem=out_recv.at[len(outward)],
+                device_id={"path": peer},
+            )
+            copy.start()
+            outward.append(copy)
+            continue
+        if not back:
+            for copy in local:
+                copy.start()
+            give_tokens.start()
+            for copy in local[:3]:
+                copy.wait()
+
+            @pl.loop(0, count)
+            def _(path):
+                own[path] = own_block(path).astype(own.dtype)
+
         copy = pltpu.make_async_remote_copy(
             src_ref=own.at[peer],
             dst_ref=returned.at[me],
-            send_sem=back_send.at[flips],
-            recv_sem=back_recv.at[flips],
+            send_sem=back_send.at[len(back)],
+            recv_sem=back_recv.at[len(back)],
             device_id={"path": peer},
         )
         copy.start()
-        back.append(copy)
+        back.append((peer, copy))
 
     share = outer_rate * (1.0 + outer_momentum)
-    for copy in local[2:]:
+    for copy in local[3:]:
         copy.wait()
     synced_ref[block_of(me), :] = (
         own_block(me) + share * weights[block_of(me), :].astype(jnp.float32)
@@ -188,7 +195,7 @@
     @pl.loop(0, count)
     def _(at):
         path = lax.fori_loop(
-            0, count, lambda i, found: jnp.where(module_ref[i] == at, i, found), jnp.int32(0)
+            0, count, lambda i, found: jnp.where(module_ref[0, i] == at, i, found), jnp.int32(0)
         )
         shaped = params[at]
         pseudo = shaped - received[path].astype(jnp.float32)
@@ -196,13 +203,36 @@
         moment_new_ref[at] = moved
         params_new_ref[at] = shaped - outer_rate * (pseudo + outer_momentum * moved)
 
-    for flips, copy in zip(order, back):
+    for peer, copy in back:
         copy.wait()
-        peer = partner(me, count, flips)
         synced_ref[block_of(peer), :] = (
             returned[peer].astype(jnp.float32)
             + share * weights[block_of(peer), :].astype(jnp.float32)
         ).astype(synced_ref.dtype)
+
+
+def write_kernel(*refs):
+    sources, targets, sem = refs[:5], refs[5:10], refs[10]
+    copies = [
+        pltpu.make_async_copy(source, target, sem.at[i])
+        for i, (source, target) in enumerate(zip(sources, targets))
+    ]
+    for copy in copies:
+        copy.start()
+    for copy in copies:
+        copy.wait()
+
+
+def write(*arrays):
+    anywhere = pl.BlockSpec(memory_space=pl.ANY)
+    return pl.pallas_call(
+        write_kernel,
+        in_specs=[anywhere] * 5,
+        out_specs=[anywhere] * 5,
+        out_shape=[jax.ShapeDtypeStruct(array.shape, array.dtype) for array in arrays],
+        scratch_shapes=[pltpu.SemaphoreType.DMA((5,))],
+        compiler_params=pltpu.CompilerParams(vmem_limit_bytes=2**20),
+    )(*arrays)
 
 
 def fused(features, weights_here, cotangent, path_module, outer_params, outer_moment):
@@ -211,9 +241,9 @@
     tokens, half = features.shape
     anywhere = pl.BlockSpec(memory_space=pl.ANY)
     sixteen = jnp.bfloat16
-    return pl.pallas_call(
+    results = pl.pallas_call(
         functools.partial(fused_kernel, count),
-        in_specs=[pl.BlockSpec(memory_space=pltpu.SMEM)] + [anywhere] * 5,
+        in_specs=[anywhere] * 6,
         out_specs=[pl.BlockSpec(memory_space=pltpu.VMEM)] * 5,
         out_shape=[
             pltpu.VMEM((depth, columns), sixteen),
@@ -223,6 +253,7 @@
             pltpu.VMEM((tokens, half), sixteen),
         ],
         scratch_shapes=[
+            pltpu.SMEM((1, count), jnp.int32),
             pltpu.VMEM((2, tokens, half), sixteen),
             pltpu.VMEM((depth, columns), sixteen),
             pltpu.VMEM((tokens, columns), sixteen),
@@ -233,7 +264,7 @@
             pltpu.VMEM(outer_params.shape, sixteen),
             pltpu.VMEM((2, tokens, half), jnp.float32),
             pltpu.VMEM((tokens, half), jnp.float32),
-            pltpu.SemaphoreType.DMA((6,)),
+            pltpu.SemaphoreType.DMA((7,)),
             pltpu.SemaphoreType.DMA((count,)),
             pltpu.SemaphoreType.DMA((count,)),
             pltpu.SemaphoreType.DMA((count,)),
@@ -244,7 +275,8 @@
         compiler_params=pltpu.CompilerParams(
             collective_id=0, has_side_effects=True, vmem_limit_bytes=40 * 2**20
         ),
-    )(path_module[:, 0], features, weights_here, cotangent, outer_params, outer_moment)
+    )(path_module.reshape(1, count), features, weights_here, cotangent, outer_params, outer_moment)
+    return write(*[pltpu.with_memory_space_constraint(x, pltpu.VMEM) for x in results])
 
 
 def many_paths_each(weights_here, path_module, outer_params, outer_moment):

time: 125 us -> 115 us (0.920)
  local copies, waits for them, and re-layouts: 8.58 us -> 0.65 us
  Pallas kernels: 115 us -> 113 us
    unnamed x7 -> x2, local copies, waits for them, and re-layouts: 8.58 us -> 0.65 us
    pallas_call x1 -> x2, Pallas kernels: 115 us -> 113 us  [the longest x1 108 us: fused(): pl.pallas_call(functools.partial(fused_kernel, count), in_specs=[anywhere...]
where the time goes in v2:
time: 115 us; the launch traced here: 114 us
  Pallas kernels  113 us (98%)
    pallas_call x1, Pallas kernels, fused(): pl.pallas_call(functools.partial(fused_kernel, count), in_specs=[anywhere...  108 us
    pallas_call x1, Pallas kernels, write(): pl.pallas_call(write_kernel, in_specs=[anywhere] * 5, out_specs=[anywhere...  5.25 us

profile of v2, /device:TPU:12, one launch (start us, length us, event | category | flops | bytes accessed | tf_op | source)
XLA Modules:
  0.0 114.1 jit_solution(6116309114399486292)
XLA Ops:
  0.6 0.0 copy-start
  0.6 0.6 copy-done
  1.3 107.5 %shard_map.101 = (bf16[768,1536]{1,0:T(8,128)(2,1)S(1)}, f32[16,48,1536]{2,1,0:T(8,128)S(1)}, f32[16,48,1536]{2,1,0:T(8,128)S(1)}, bf16[768,1536]{1,0:T(8,128)(2,1)S(1)}, bf16[512,384]{1,0:T(8,128)(2,1)S(1)}) custom-call(s32[1,16]{1,0:T(1,128)S(1)} %bitcast.7, bf16[512,384]{1,0:T(8,128)(2,1)} %bitcast.10, bf16[768,1536]{1,0:T(8,128)(2,1)} %bitcast.8, ...), custom_call_target="tpu_custom_call" | custom-call | tf_op jit(solution)/shard_map/pallas_call | solution.py:244
  108.8 5.3 %shard_map.102 = (bf16[768,1536]{1,0:T(8,128)(2,1)}, f32[16,48,1536]{2,1,0:T(8,128)}, f32[16,48,1536]{2,1,0:T(8,128)}, bf16[768,1536]{1,0:T(8,128)(2,1)}, bf16[512,384]{1,0:T(8,128)(2,1)}) custom-call(bf16[768,1536]{1,0:T(8,128)(2,1)S(1)} %get-tuple-element.15.refs_0_, f32[16,48,1536]{2,1,0:T(8,128)S(1)} %get-tuple-element.16.refs_1_, ...), custom_call_target="tpu_custom_call" | custom-call | tf_op jit(solution)/shard_map/pallas_call | solution.py:228
Async XLA Ops:
  0.6 0.7 copy-start
